TPU v7x, 256 devices: a whole 4x4x8 slice. The times are simulated.
256 devices in a mesh: dp: 32 (over z, y_hi, core), expert: 8 (over y_lo, x).
Axes of the slice: x: 4, y: 4 (y_hi: 2, y_lo: 2; y = y_hi * 2 + y_lo), z: 8, core: 2. Of those that a mesh axis runs over, the one named last changes fastest.
Arguments:
- tokens: bfloat16 [1024, 7168], P('dp', 'expert'), may hold values from -6 to 6
- cotangent: bfloat16 [1024, 7168], P('dp', 'expert'), may hold values from -0.75 to 0.75
- route_ids: int32 [1024, 2], replicated, may hold values from 0 to 3, all different within a row; in each aligned block of 1024 rows (0 to 1023, 1024 to 2047, ...) at most 640 rows name the same one
- route_probs: float32 [1024, 2], replicated, may hold values from 0.25 to 1
- dense_gate: bfloat16 [7168, 4864], P('expert', 'dp'), may hold values from -0.0625 to 0.0625
- dense_up: bfloat16 [7168, 4864], P('expert', 'dp'), may hold values from -0.0625 to 0.0625
- dense_down: bfloat16 [4864, 7168], P('dp', 'expert'), may hold values from -0.078125 to 0.078125
- expert_gate: bfloat16 [7168, 19456], P('expert', 'dp'), may hold values from -0.0625 to 0.0625
- expert_up: bfloat16 [7168, 19456], P('expert', 'dp'), may hold values from -0.0625 to 0.0625
- expert_down: bfloat16 [19456, 7168], P('dp', 'expert'), may hold values from -0.078125 to 0.078125
Outputs:
- input_grad: float32 [1024, 7168], P('dp', 'expert')
- dense_gate_grad: float32 [7168, 4864], P('expert', 'dp')
- dense_up_grad: float32 [7168, 4864], P('expert', 'dp')
- dense_down_grad: float32 [4864, 7168], P('dp', 'expert')
- expert_gate_grad: float32 [7168, 19456], P('expert', 'dp')
- expert_up_grad: float32 [7168, 19456], P('expert', 'dp')
- expert_down_grad: float32 [19456, 7168], P('dp', 'expert')
Inputs may be any that keep to these rules, and one draw needn't show every extreme that they name: `route_ids`: each row names two different experts; no expert is named by more than 640 rows, a bound that some block reaches.
All inputs are finite; a program needn't handle non-finite values.
Results may differ from a plain program's by a relative error of at most 0.0029.
Values may be sent and summed in bfloat16 or wider, within the bound.
No kernel may reach another device: no remote copies, remote signals or barrier semaphores. Data moves between devices by JAX's collectives and lax.ppermute only.
A program may use at most 128 MiB of HBM per device.

v0:
```python
import jax
import jax.numpy as jnp
from jax import lax
from jax.sharding import PartitionSpec as P

FF = 4864


def slot_table(route_ids, route_probs, expert_number, capacity):
    chosen = route_ids == expert_number
    member = jnp.any(chosen, axis=1)
    token_weight = jnp.sum(jnp.where(chosen, route_probs, jnp.zeros_like(route_probs)), axis=1)
    position = jnp.cumsum(member.astype(jnp.int32)) - 1
    target = jnp.where(member, position, capacity)
    order = jnp.arange(route_ids.shape[0], dtype=jnp.int32)
    slot_token = jnp.zeros((capacity,), jnp.int32).at[target].set(order, mode="drop")
    slot_weight = (
        jnp.zeros((capacity,), route_probs.dtype).at[target].set(token_weight, mode="drop")
    )
    return (slot_token, slot_weight)


def swiglu_terms(gate_part, up_part, back_part, weight):
    sigmoid_gate = jax.nn.sigmoid(gate_part)
    lifted = gate_part * sigmoid_gate
    weighted = (weight * lifted * up_part).astype(jnp.bfloat16)
    grad_act = weight * back_part
    grad_gate = (
        grad_act * up_part * sigmoid_gate * (1.0 + gate_part * (1.0 - sigmoid_gate))
    ).astype(jnp.bfloat16)
    grad_up = (grad_act * lifted).astype(jnp.bfloat16)
    return (weighted, grad_gate, grad_up)


def over_rows(left, right):
    return lax.dot_general(
        left, right, (((0,), (0,)), ((), ())), preferred_element_type=jnp.float32
    )


def over_cols(left, right):
    return lax.dot_general(
        left, right, (((1,), (1,)), ((), ())), preferred_element_type=jnp.float32
    )


def shards(
    tokens,
    cotangent,
    route_ids,
    route_probs,
    dense_gate,
    dense_up,
    dense_down,
    expert_gate,
    expert_up,
    expert_down,
):
    all_tokens, all_grads = (
        lax.all_gather(tokens, "dp", axis=0, tiled=True),
        lax.all_gather(cotangent, "dp", axis=0, tiled=True),
    )
    total_rows = all_tokens.shape[0]
    capacity = 5 * total_rows // 8
    piece_width = expert_gate.shape[1]
    expert_number = lax.axis_index("dp") * piece_width // FF
    slot_token, slot_weight = slot_table(route_ids, route_probs, expert_number, capacity)
    rows_in = jnp.take(all_tokens, slot_token, axis=0)
    rows_back = jnp.take(all_grads, slot_token, axis=0)
    gate_dense = jnp.dot(all_tokens, dense_gate, preferred_element_type=jnp.float32)
    up_dense = jnp.dot(all_tokens, dense_up, preferred_element_type=jnp.float32)
    back_dense = over_cols(all_grads, dense_down)
    gate_rows = jnp.dot(rows_in, expert_gate, preferred_element_type=jnp.float32)
    up_rows = jnp.dot(rows_in, expert_up, preferred_element_type=jnp.float32)
    back_rows = over_cols(rows_back, expert_down)
    summed = lax.psum((gate_rows, up_rows, back_rows, gate_dense, up_dense, back_dense), "expert")
    weighted_e, grad_gate_e, grad_up_e = swiglu_terms(
        summed[0], summed[1], summed[2], slot_weight[:, None]
    )
    weighted_d, grad_gate_d, grad_up_d = swiglu_terms(summed[3], summed[4], summed[5], 1.0)
    dense_gate_grad = over_rows(all_tokens, grad_gate_d)
    dense_up_grad = over_rows(all_tokens, grad_up_d)
    dense_down_grad = over_rows(weighted_d, all_grads)
    expert_gate_grad = over_rows(rows_in, grad_gate_e)
    expert_up_grad = over_rows(rows_in, grad_up_e)
    expert_down_grad = over_rows(weighted_e, rows_back)
    dense_input = over_cols(grad_gate_d, dense_gate) + over_cols(grad_up_d, dense_up)
    expert_input = over_cols(grad_gate_e, expert_gate) + over_cols(grad_up_e, expert_up)
    combined = dense_input.at[slot_token].add(expert_input)
    input_grad = lax.psum_scatter(combined, "dp", scatter_dimension=0, tiled=True)
    return (
        input_grad,
        dense_gate_grad,
        dense_up_grad,
        dense_down_grad,
        expert_gate_grad,
        expert_up_grad,
        expert_down_grad,
    )


def solution(mesh):
    in_specs = (
        P("dp", "expert"),
        P("dp", "expert"),
        P(),
        P(),
        P("expert", "dp"),
        P("expert", "dp"),
        P("dp", "expert"),
        P("expert", "dp"),
        P("expert", "dp"),
        P("dp", "expert"),
    )
    out_specs = (
        P("dp", "expert"),
        P("expert", "dp"),
        P("expert", "dp"),
        P("dp", "expert"),
        P("expert", "dp"),
        P("expert", "dp"),
        P("dp", "expert"),
    )
    return jax.shard_map(shards, mesh=mesh, in_specs=in_specs, out_specs=out_specs, check_vma=False)
```

profile of v0, /device:TPU:2, one launch (start us, length us, event | category | flops | bytes accessed | tf_op | source)
XLA Modules:
  0.0 499.2 jit_solution(10703919760621852359)
XLA Ops:
  7.2 0.7 all-gather.5.cloned.1.call-update
  8.0 0.7 all-gather.3.cloned.1.call-update
  8.7 0.7 fusion.18
  10.1 4.3 scatter_custom_fusion
  14.4 78.6 %all-gather.5.cloned.1.call-done = bf16[1024,896]{1,0:T(8,128)(2,1)} async-done(((bf16[32,896]{1,0:T(8,128)(2,1)}), bf16[1024,896]{1,0:T(8,128)(2,1)}) %all-gather.5.cloned.1.call-update) | async-done | bytes 1835024 | tf_op jit(solution)/shard_map/all_gather | solution.py:60
  93.0 5.6 %gather_fusion.1 = bf16[640,896]{1,0:T(8,128)(2,1)S(1)} fusion(bf16[1024,896]{1,0:T(8,128)(2,1)} %all-gather.5.cloned.1.call-done, s32[1024]{0:T(1024)S(1)} %pad_clamp_fusion), kind=kCustom, calls=%fused_computation.1.clone | custom fusion | bytes 2296320 | tf_op jit(solution)/shard_map/jit(_take)/gather | solution.py:68
  98.6 2.4 fusion.21
  101.0 2.4 fusion.22
  103.4 68.2 %all-gather.3.cloned.1.call-done = bf16[1024,896]{1,0:T(8,128)(2,1)} async-done(((bf16[32,896]{1,0:T(8,128)(2,1)}), bf16[1024,896]{1,0:T(8,128)(2,1)}) %all-gather.3.cloned.1.call-update) | async-done | bytes 1835024 | tf_op jit(solution)/shard_map/all_gather | solution.py:61
  171.6 5.6 %gather_fusion = bf16[640,896]{1,0:T(8,128)(2,1)S(1)} fusion(bf16[1024,896]{1,0:T(8,128)(2,1)} %all-gather.3.cloned.1.call-done, s32[1024]{0:T(1024)S(1)} %pad_clamp_fusion), kind=kCustom, calls=%fused_computation.clone | custom fusion | bytes 2296320 | tf_op jit(solution)/shard_map/jit(_take)/gather | solution.py:69
  177.2 1.0 copy-done.8
  178.2 3.7 fusion.6
  182.0 1.7 fusion.23
  183.6 1.7 fusion.25
  185.3 1.7 fusion.24
  187.1 0.6 copy-done.24
  187.7 4.5 scatter_custom_fusion.1
  192.2 145.9 %all-reduce.3.cloned.1.call-done = (f32[1024,152]{0,1:T(8,128)}, f32[1024,152]{0,1:T(8,128)}, f32[1024,152]{0,1:T(8,128)}, f32[640,608]{0,1:T(8,128)}, f32[640,608]{0,1:T(8,128)}, /*index=5*/f32[640,608]{0,1:T(8,128)}) async-done(((f32[1024,152]{0,1:T(8,128)}, f32[1024,152]{0,1:T(8,128)}, f32[1024,152]{0,1:T(8,128)}, f32[640,608]{0,1:T(8,128)}, f32[640,608]{0,1:T(8,128)}, /*index=5*/f32[640,608]{0,1:T(8,128)}), ...) | async-done | bytes 6537232 | tf_op jit(solution)/shard_map/psum | solution.py:76
  338.2 3.1 multiply_convert_fusion.1
  341.3 2.6 fusion.27
  343.9 2.6 fusion.28
  346.9 0.6 copy-done.13
  347.5 0.8 fusion.26
  348.4 2.5 convolution_add_fusion
  351.0 14.9 %scatter_custom_fusion.2 = f32[1024,896]{1,0:T(8,128)} fusion(f32[1024,896]{1,0:T(8,128)} %convolution_add_fusion, s32[640]{0:T(1024)S(1)} %compare_select_fusion.1, f32[640,896]{1,0:T(8,128)} %fusion.27, f32[640,896]{1,0:T(8,128)} %fusion.28), kind=kCustom, calls=%fused_computation.5 | custom fusion | flops 1146880 | bytes 8257536 | tf_op jit(solution)/shard_map/scatter-add | solution.py:89
  365.9 1.3 convolution_bitcast_fusion
  367.2 1.3 convolution_bitcast_fusion.1
  369.1 1.4 fusion.7
  370.5 2.6 fusion.20
  373.1 2.6 fusion.19
  375.7 2.7 fusion.3
  378.4 114.3 %reduce-scatter.2.cloned.1.call-done = f32[32,896]{1,0:T(8,128)} async-done(((f32[1024,896]{1,0:T(8,128)}), f32[32,896]{1,0:T(8,128)}) %reduce-scatter.2.cloned.1.call-update) | async-done | bytes 114704 | tf_op jit(solution)/shard_map/reduce_scatter | solution.py:90
  (76 shorter events, 2.1 us)
Async XLA Ops:
  7.2 91.4 %copy-start = (bf16[896,608]{0,1:T(8,128)(2,1)S(1)}, bf16[896,608]{0,1:T(8,128)(2,1)}, u32[]{:S(2)}) copy-start(bf16[896,608]{0,1:T(8,128)(2,1)} %param.19) | copy-start | bytes 3268612
  7.2 85.9 %all-gather.5.cloned.1.call-start = ((), (), s32[]{:S(2)}) async-start(), calls=%async_computation.2 | async-start | bytes 1892352 | tf_op jit(solution)/shard_map/all_gather | solution.py:60
  7.9 163.7 %all-gather.3.cloned.1.call-start = ((), (), s32[]{:S(2)}) async-start(), calls=%async_computation.1 | async-start | bytes 1892352 | tf_op jit(solution)/shard_map/all_gather | solution.py:61
  8.7 329.5 %all-reduce.3.cloned.1.call-start = ((), (), s32[]{:S(2)}) async-start(), calls=%async_computation.4 | async-start | bytes 13074432 | tf_op jit(solution)/shard_map/psum | solution.py:76
  14.4 162.8 %copy-start.26 = (pred[640]{0:T(1024)(128)(4,1)}, pred[640]{0:T(1024)(128)(4,1)S(1)}, u32[]{:S(2)}) copy-start(pred[640]{0:T(1024)(128)(4,1)S(1)} %compare_and_fusion) | copy-start | bytes 1924
  98.6 2.4 copy-start.6
  98.6 2.4 copy-start.28
  177.2 1.0 copy-start.8
  178.2 3.8 copy-start.2
  178.2 3.8 copy-start.23
  182.0 1.7 copy-start.1
  182.0 1.7 copy-start.12
  183.6 1.7 copy-start.10
  187.0 305.6 %reduce-scatter.2.cloned.1.call-start = ((), (), s32[]{:S(2)}) async-start(), calls=%async_computation.3 | async-start | bytes 3784704 | tf_op jit(solution)/shard_map/reduce_scatter | solution.py:90
  341.3 2.6 copy-start.14
  341.3 2.6 copy-start.16
  341.3 2.6 copy-start.29
  343.9 2.6 copy-start.18
  343.9 2.6 copy-start.20
  343.9 2.6 copy-start.22
  346.5 1.0 copy-start.13
  347.5 1.0 copy-start.11
  365.9 2.6 copy-start.21
  367.2 1.6 copy-start.3
  367.2 1.8 copy-start.19
  369.0 1.4 copy-start.7
  369.0 1.5 copy-start.17
  369.1 1.5 copy-start.27
  370.5 2.6 copy-start.15
  373.1 2.6 copy-start.4
  373.1 2.6 copy-start.5
  373.1 2.6 copy-start.9
  (2 other events, 1.4 us)
Sparse Core Ops, SparseCore 0:
  10.8 82.2 all-gather.4
  95.8 75.7 all-gather.2
  187.1 150.9 all-reduce.2
  366.0 126.5 reduce-scatter.1
where the time goes:
time: 500 us; the launch traced here: 499 us
  waiting for transfers between devices  408 us (82%)
  matrix products  33.8 us (7%)
  local copies, waits for them, and re-layouts  23.2 us (5%)
  other arithmetic  19.5 us (4%)
  between operations  14 us (3%)
    psum x1, waiting for transfers between devices, shards(): lax.psum((gate_rows, up_rows, back_rows, gate_dense, up_dense, back_dense...  146 us
    reduce_scatter x1, waiting for transfers between devices, shards(): lax.psum_scatter(combined, 'dp', scatter_dimension=0, tiled=True)  114 us
    all_gather x1, waiting for transfers between devices, shards(): lax.all_gather(tokens, 'dp', axis=0, tiled=True)  78.6 us
    all_gather x1, waiting for transfers between devices, shards(): lax.all_gather(cotangent, 'dp', axis=0, tiled=True)  68.2 us
    scatter-add x1, other arithmetic, shards(): combined = dense_input.at[slot_token].add(expert_input)  14.9 us
    dot_general x6, matrix products, over_cols(): lax.dot_general(left, right, (((1,), (1,)), ((), ())), preferred_element_...  13.9 us
    dot_general x6, matrix products, over_rows(): lax.dot_general(left, right, (((0,), (0,)), ((), ())), preferred_element_...  11.8 us
  transfers between devices with their start and end apart: 4, of which 4 were waited for; matrix products, arithmetic and copies ran while one was open for 6% of the time, Pallas kernels for 0%

commit v1 on v0

v1 whole, which is shorter than its diff:
```python
import jax
import jax.numpy as jnp
from jax import lax
from jax.experimental import pallas as pl
from jax.experimental.pallas import tpu as pltpu
from jax.sharding import Mesh, PartitionSpec as P

FF = 4864
Z, YH, C, YL, X = 8, 2, 2, 2, 4
AXES = ("z", "yh", "c", "yl", "x")
SIZES = (Z, YH, C, YL, X)
DP = ("z", "yh", "c")
EX = ("yl", "x")
PARTS = YL * X
F32 = jnp.float32
BF16 = jnp.bfloat16
TOKENS, CAP, WIDTH = 1024, 640, 896
HE, HD = 608, 152
QUARTER = 256
STRIDE = 160
SHARE = 80
BLOCK = 3 * SHARE
CODED = BLOCK + 16
OWN = 32
VMEM = 40 * 1024 * 1024


def dot(left, right, dims):
    return lax.dot_general(left, right, ((dims[:1], dims[1:]), ((), ())), preferred_element_type=F32)


def shape(dims, kind):
    return jax.ShapeDtypeStruct(dims, kind)


def shift(value, axis, size, step):
    return lax.ppermute(value, axis, [(i, (i + step) % size) for i in range(size)])


def gather_column(own):
    pair = jnp.stack([own, shift(own, "yh", YH, 1)])
    pieces = [pair]
    below, above = pair, pair
    for _ in range(Z // 2 - 1):
        below, above = shift(below, "z", Z, 1), shift(above, "z", Z, -1)
        pieces += [below, above]
    pieces += [shift(below[:1], "z", Z, 1), shift(above[1:], "z", Z, -1)]
    return jnp.concatenate(pieces)


def gather_terms(value, first):
    if first == "x":
        near = [value, shift(value, "x", X, 1), shift(value, "x", X, -1), shift(value, "x", X, 2)]
        return [v[None] for v in near + [shift(v, "yl", YL, 1) for v in near]]
    pair = jnp.stack([value, shift(value, "yl", YL, 1)])
    return [pair, shift(pair, "x", X, 1), shift(pair, "x", X, -1), shift(pair, "x", X, 2)]


FROM_X = (0, -1, 1, 2)
RELATIVE = {
    "x": [[(r, k)] for r in range(YL) for k in FROM_X],
    "yl": [[(0, k), (1, k)] for k in FROM_X],
}
FROM_Z = (0, -1, 1, -2, 2, -3, 3, 4)


def place_terms(place_ref, blocks, first, to_ref):
    yl, x = place_ref[3], place_ref[4]
    for block, origins in zip(blocks, RELATIVE[first]):
        for i, (row, away) in enumerate(origins):
            j = lax.rem(yl + row, YL) * X + lax.rem(x + away + X, X)
            to_ref[pl.ds(pl.multiple_of(j * SHARE, SHARE), SHARE), :] = block[i]


def forward_kernel(place_ref, pos_ref, mine_ref, sibling_ref, *refs):
    far_weights, far_rows, out_ref = refs[:6], refs[6:10], refs[10]
    weights, rows, sums_ref, in_sems, out_sems = refs[11:17], refs[17:21], refs[21], refs[22], refs[23]
    tok_ref, cot_ref, in_ref, back_ref = rows
    weights_e, weights_d = weights[0:6:2], weights[1:6:2]
    fetches = [pltpu.make_async_copy(far, near, in_sems.at[i]) for i, (far, near) in enumerate(zip(far_weights, weights))]
    stores = [pltpu.make_async_copy(near, far, out_sems.at[i]) for i, (near, far) in enumerate(zip(rows, far_rows))]
    for fetch in fetches:
        fetch.start()
    z, yh, c = place_ref[0], place_ref[1], place_ref[2]
    for core, column in enumerate((mine_ref, sibling_ref)):
        for k, away in enumerate(FROM_Z):
            for r in range(YH):
                at = lax.rem(z + away + Z, Z) * (YH * C * OWN) + lax.rem(yh + r, YH) * (C * OWN) + lax.rem(c + core, C) * OWN
                at = pl.multiple_of(at, OWN)
                tok_ref[pl.ds(at, OWN), :] = column[YH * k + r, 0]
                cot_ref[pl.ds(at, OWN), :] = column[YH * k + r, 1]
    slots = lax.broadcasted_iota(jnp.int32, (CAP, TOKENS), 0)
    one_hot = jnp.where(slots == pos_ref[...], 1.0, 0.0).astype(BF16)
    in_ref[...] = dot(one_hot, tok_ref[...], (1, 0)).astype(BF16)
    back_ref[...] = dot(one_hot, cot_ref[...], (1, 0)).astype(BF16)
    for store in stores:
        store.start()
    exponents = [[] for _ in range(PARTS)]
    for k in range(3):
        picked, whole = (back_ref, cot_ref) if k == 2 else (in_ref, tok_ref)
        fetches[2 * k].wait()
        fetches[2 * k + 1].wait()
        sums_ref[0:HE, 0:CAP] = dot(weights_e[k][...], picked[...], (1, 1))
        sums_ref[HE:, 0:CAP] = jnp.zeros((PARTS * SHARE - HE, CAP), F32)
        dense = dot(weights_d[k][...], whole[...], (1, 1))
        for q in range(TOKENS // QUARTER):
            sums_ref[q * STRIDE : q * STRIDE + HD, CAP:] = dense[:, q * QUARTER : (q + 1) * QUARTER]
            sums_ref[q * STRIDE + HD : (q + 1) * STRIDE, CAP:] = jnp.zeros((STRIDE - HD, QUARTER), F32)
        for j in range(PARTS):
            block = sums_ref[j * SHARE : (j + 1) * SHARE, :]
            largest = jnp.maximum(jnp.max(jnp.abs(block), axis=0, keepdims=True), 1e-30)
            exponent = jnp.ceil(jnp.log2(largest) + 1e-3)
            coded = jnp.round(block * jnp.exp2(15.0 - exponent))
            coded = jnp.minimum(jnp.maximum(coded, -32767.0), 32767.0)
            out_ref[j, k * SHARE : (k + 1) * SHARE, :] = coded.astype(jnp.int32).astype(jnp.int16)
            exponents[j].append(exponent)
    row = lax.broadcasted_iota(jnp.int32, (CODED - BLOCK, WIDTH), 0)
    for j in range(PARTS):
        tile = jnp.where(row == 0, exponents[j][0], jnp.where(row == 1, exponents[j][1], exponents[j][2]))
        out_ref[j, BLOCK:, :] = tile.astype(jnp.int32).astype(jnp.int16)
    for store in stores:
        store.wait()


def terms_kernel(in_ref, weight_ref, weighted_ref, gate_ref, up_ref):
    totals = []
    for k in range(3):
        total = jnp.zeros((SHARE, WIDTH), F32)
        for j in range(PARTS):
            exponent = in_ref[j, BLOCK:, :].astype(jnp.int32).astype(F32)[k : k + 1]
            total = total + in_ref[j, k * SHARE : (k + 1) * SHARE, :].astype(jnp.int32).astype(F32) * jnp.exp2(exponent - 15.0)
        totals.append(total)
    gate, up, back = totals
    weight = weight_ref[...]
    sigmoid_gate = 1.0 / (1.0 + jnp.exp(-gate))
    lifted = gate * sigmoid_gate
    grad_act = weight * back
    weighted_ref[...] = (weight * lifted * up).astype(BF16)
    gate_ref[...] = (grad_act * up * sigmoid_gate * (1.0 + gate * (1.0 - sigmoid_gate))).astype(BF16)
    up_ref[...] = (grad_act * lifted).astype(BF16)


def input_kernel(place_ref, pos_ref, *refs):
    blocks, refs = refs[:12], refs[12:]
    gate_e, gate_d, up_e, up_d, kept_ref, sent_ref, gate_ref, up_ref, total_ref = refs
    c = place_ref[2]
    place_terms(place_ref, blocks[:8], "x", gate_ref)
    place_terms(place_ref, blocks[8:], "yl", up_ref)
    gate, up = gate_ref[...], up_ref[...]
    routed = dot(gate[0:HE, 0:CAP], gate_e[...], (0, 0)) + dot(up[0:HE, 0:CAP], up_e[...], (0, 0))
    high = routed.astype(BF16)
    low = (routed - high.astype(F32)).astype(BF16)
    slots = lax.broadcasted_iota(jnp.int32, (TOKENS, CAP), 1)
    one_hot = jnp.where(slots == pos_ref[...], 1.0, 0.0).astype(BF16)
    total_ref[...] = dot(one_hot, high, (1, 0)) + dot(one_hot, low, (1, 0))
    for q in range(TOKENS // QUARTER):
        rows = slice(q * STRIDE, q * STRIDE + HD)
        dense = dot(gate[rows, CAP:], gate_d[...], (0, 0)) + dot(up[rows, CAP:], up_d[...], (0, 0))
        total_ref[q * QUARTER : (q + 1) * QUARTER, :] += dense
    for i in range(Z * YH):
        mine = pl.multiple_of(i * C * OWN + c * OWN, OWN)
        other = pl.multiple_of(i * C * OWN + (1 - c) * OWN, OWN)
        kept_ref[i] = total_ref[pl.ds(mine, OWN), :]
        sent_ref[i] = total_ref[pl.ds(other, OWN), :].astype(BF16)


def weights_kernel(place_ref, gate_ref, up_ref, *refs):
    blocks, (tok_ref, cot_ref, in_ref, back_ref), outs, down_ref = refs[:4], refs[4:8], refs[8:14], refs[14]
    place_terms(place_ref, blocks, "yl", down_ref)
    for k, (value_ref, rows, whole) in enumerate(((gate_ref, in_ref, tok_ref), (up_ref, in_ref, tok_ref), (down_ref, back_ref, cot_ref))):
        dense = jnp.concatenate([value_ref[q * STRIDE : q * STRIDE + HD, CAP:] for q in range(TOKENS // QUARTER)], axis=1)
        outs[k][...] = dot(dense, whole[...], (1, 0))
        outs[k + 3][...] = dot(value_ref[0:HE, 0:CAP], rows[...], (1, 0))


def shards(tokens, cotangent, route_ids, route_probs, dense_gate, dense_up, dense_down, expert_gate, expert_up, expert_down):
    expert_number = lax.axis_index(DP) * HE // FF
    place = jnp.stack([lax.axis_index(a) for a in AXES]).astype(jnp.int32)
    smem = pl.BlockSpec(memory_space=pltpu.SMEM)

    chosen = route_ids == expert_number
    member = jnp.any(chosen, axis=1)
    token_weight = jnp.sum(jnp.where(chosen, route_probs, 0.0), axis=1)
    position = jnp.where(member, jnp.cumsum(member.astype(jnp.int32)) - 1, -1)
    slots = lax.broadcasted_iota(jnp.int32, (CAP, TOKENS), 0)
    slot_weight = jnp.sum(jnp.where(slots == position[None, :], token_weight[None, :], 0.0), axis=1)
    weight = jnp.concatenate([slot_weight, jnp.ones((QUARTER,), F32)])[None, :]

    mine_column = gather_column(jnp.stack([tokens, cotangent]))
    across, down = lax.optimization_barrier((position[None, :], position[:, None]))
    sibling_column = shift(mine_column, "c", C, 1)
    gate_e, gate_d, up_e, up_d = expert_gate.T, dense_gate.T, expert_up.T, dense_up.T

    far, vmem = pl.BlockSpec(memory_space=pl.ANY), pl.BlockSpec(memory_space=pltpu.VMEM)
    params = pltpu.CompilerParams(vmem_limit_bytes=VMEM)
    small, large = (HD, WIDTH), (HE, WIDTH)
    whole, picked, share = (TOKENS, WIDTH), (CAP, WIDTH), (SHARE, WIDTH)
    held = [(large, BF16), (small, BF16)] * 3 + [(whole, BF16)] * 2 + [(picked, BF16)] * 2
    all_tokens, all_grads, rows_in, rows_back, coded = pl.pallas_call(
        forward_kernel,
        out_shape=[shape(*h) for h in held[6:]] + [shape((PARTS, CODED, WIDTH), jnp.int16)],
        in_specs=[smem, vmem, vmem, vmem] + [far] * 6,
        out_specs=[far] * 4 + [vmem],
        scratch_shapes=[pltpu.VMEM(*h) for h in held]
        + [pltpu.VMEM((PARTS * SHARE, WIDTH), F32), pltpu.SemaphoreType.DMA((6,)), pltpu.SemaphoreType.DMA((4,))],
        compiler_params=params,
        name="forward",
    )(place, across, mine_column, sibling_column, gate_e, gate_d, up_e, up_d, expert_down, dense_down)
    arrived = lax.all_to_all(coded, EX, 0, 0)
    weighted, grad_gate, grad_up = pl.pallas_call(
        terms_kernel,
        out_shape=[shape(share, BF16)] * 3,
        compiler_params=params,
        name="terms",
    )(arrived, weight)

    part = (Z * YH, OWN, WIDTH)
    summed = (PARTS * SHARE, WIDTH)
    kept, sent, gate_terms, up_terms = pl.pallas_call(
        input_kernel,
        out_shape=[shape(part, F32), shape(part, BF16), shape(summed, BF16), shape(summed, BF16)],
        in_specs=[smem] + [vmem] * 17,
        scratch_shapes=[pltpu.VMEM(whole, F32)],
        compiler_params=params,
        name="input",
    )(place, down, *gather_terms(grad_gate, "x"), *gather_terms(grad_up, "yl"), gate_e, gate_d, up_e, up_d)
    sent, weighted = lax.optimization_barrier((sent, weighted))
    chip = (kept + shift(sent, "c", C, 1).astype(F32)).astype(BF16)
    weighted_terms = gather_terms(weighted, "yl")
    input_grad = jnp.sum(lax.all_to_all(chip, ("z", "yh"), 0, 0).astype(F32), axis=0)

    grads = pl.pallas_call(
        weights_kernel,
        out_shape=[shape(small, F32)] * 3 + [shape(large, F32)] * 3,
        in_specs=[smem] + [vmem] * 10,
        scratch_shapes=[pltpu.VMEM(summed, BF16)],
        compiler_params=params,
        name="weights",
    )(place, gate_terms, up_terms, *weighted_terms, all_tokens, all_grads, rows_in, rows_back)
    return (input_grad, grads[0].T, grads[1].T, grads[2], grads[3].T, grads[4].T, grads[5])


def solution(mesh):
    fine = Mesh(mesh.devices.reshape(SIZES), AXES)
    rows, cols = P(DP, EX), P(EX, DP)
    in_specs = (rows, rows, P(), P(), cols, cols, rows, cols, cols, rows)
    out_specs = (rows, cols, cols, rows, cols, cols, rows)
    return jax.shard_map(shards, mesh=fine, in_specs=in_specs, out_specs=out_specs, check_vma=False)
```

time: 500 us -> 209 us (0.42)
  waiting for transfers between devices: 408 us -> 94.8 us
  starting transfers between devices: 0.16 us -> 52.8 us
  matrix products: 33.8 us -> 0 us
  Pallas kernels: 0 us -> 30.8 us
  between operations: 14 us -> 0.85 us
  other arithmetic: 19.5 us -> 7.59 us
    all_gather x2 -> x0, waiting for transfers between devices: 147 us -> none  [the longest x1 78.6 us: shards(): lax.all_gather(tokens, 'dp', axis=0, tiled=True)]
    psum x1 -> x0, waiting for transfers between devices: 146 us -> none  [shards(): lax.psum((gate_rows, up_rows, back_rows, gate_dense, up_dense, back_dense...]
    reduce_scatter x1 -> x0, waiting for transfers between devices: 114 us -> none  [shards(): lax.psum_scatter(combined, 'dp', scatter_dimension=0, tiled=True)]
    all_to_all x0 -> x2, waiting for transfers between devices: none -> 51.6 us  [the longest x1 51.6 us: shards(): arrived = lax.all_to_all(coded, EX, 0, 0)]
    ppermute x0 -> x26, waiting for transfers between devices: none -> 43.2 us  [shift(): lax.ppermute(value, axis, [(i, (i + step) % size) for i in range(size)])]
    ppermute x0 -> x26, starting transfers between devices: none -> 38.3 us  [shift(): lax.ppermute(value, axis, [(i, (i + step) % size) for i in range(size)])]
    dot_general x16 -> x0, matrix products: 33.8 us -> none  [the longest x6 13.9 us: over_cols(): lax.dot_general(left, right, (((1,), (1,)), ((), ())), preferred_element_...]
    pallas_call x0 -> x4, Pallas kernels: none -> 30.8 us  [the longest x1 13.8 us: shards(): pl.pallas_call(forward_kernel, out_shape=[shape(*h) for h in held[6:]] +...]
  transfers between devices with their start and end apart: 4 -> 28, of which waited for: 4 -> 16; matrix products, arithmetic and copies ran while one was open for 6% -> 5% of each run, Pallas kernels for 0% -> 3%
where the time goes in v1:
time: 209 us; the launch traced here: 207 us
  waiting for transfers between devices  94.8 us (45%)
  starting transfers between devices  52.8 us (25%)
  Pallas kernels  30.8 us (15%)
  local copies, waits for them, and re-layouts  20.7 us (10%)
  other arithmetic  7.59 us (4%)
    all_to_all x1, waiting for transfers between devices, shards(): arrived = lax.all_to_all(coded, EX, 0, 0)  51.6 us
    ppermute x26, waiting for transfers between devices, shift(): lax.ppermute(value, axis, [(i, (i + step) % size) for i in range(size)])  43.2 us
    ppermute x26, starting transfers between devices, shift(): lax.ppermute(value, axis, [(i, (i + step) % size) for i in range(size)])  38.3 us
    unnamed x48, local copies, waits for them, and re-layouts  18.7 us
    pallas_call x1, Pallas kernels, shards(): pl.pallas_call(forward_kernel, out_shape=[shape(*h) for h in held[6:]] +...  13.8 us
    all_to_all x1, starting transfers between devices, shards(): lax.all_to_all(chip, ('z', 'yh'), 0, 0).astype(F32)  8.56 us
    pallas_call x1, Pallas kernels, shards(): pl.pallas_call(input_kernel, out_shape=[shape(part, F32), shape(part, BF1...  7.36 us
    pallas_call x1, Pallas kernels, shards(): pl.pallas_call(weights_kernel, out_shape=[shape(small, F32)] * 3 + [shape...  6.47 us
  transfers between devices with their start and end apart: 28, of which 16 were waited for; matrix products, arithmetic and copies ran while one was open for 5% of the time, Pallas kernels for 3%

profile of v1, /device:TPU:2, one launch (start us, length us, event | category | flops | bytes accessed | tf_op | source)
XLA Modules:
  0.0 207.5 jit_solution(16955376962344082931)
XLA Ops:
  1.5 3.3 %collective-permute-start = (bf16[2,32,896]{2,1,0:T(8,128)(2,1)S(1)}, bf16[2,32,896]{2,1,0:T(8,128)(2,1)S(1)}, u32[]{:S(2)}, u32[]{:S(2)}) collective-permute-start(bf16[2,32,896]{2,1,0:T(8,128)(2,1)S(1)} %get-tuple-element.54), channel_id=1, source_target_pairs={{0,16},{16,0},{1,17},{17,1},{2,18},{18,2},{3,19},{19,3},{4,20},{20... | collective-permute-start | bytes 344072 | tf_op jit(solution)/shard_map/ppermute | solution.py:37
  6.3 1.7 collective-permute-done
  8.0 2.0 collective-permute-start.1
  10.0 4.0 %collective-permute-start.2 = (bf16[2,2,32,896]{3,2,1,0:T(8,128)(2,1)S(1)}, bf16[2,2,32,896]{3,2,1,0:T(8,128)(2,1)S(1)}, u32[]{:S(2)}, u32[]{:S(2)}) collective-permute-start(bf16[2,2,32,896]{3,2,1,0:T(8,128)(2,1)S(1)} %pad_maximum_fusion.2), channel_id=1, source_target_pairs={{0,224},{32,0},{64,32},{96,64},{128,96},{160,128},{192,160},{224,1... | collective-permute-start | bytes 688136 | tf_op jit(solution)/shard_map/ppermute | solution.py:37
  14.7 4.0 %collective-permute-done.1 = bf16[2,2,32,896]{3,2,1,0:T(8,128)(2,1)S(1)} collective-permute-done((bf16[2,2,32,896]{3,2,1,0:T(8,128)(2,1)S(1)}, bf16[2,2,32,896]{3,2,1,0:T(8,128)(2,1)S(1)}, u32[]{:S(2)}, u32[]{:S(2)}) %collective-permute-start.1) | collective-permute-done | bytes 229408 | tf_op jit(solution)/shard_map/ppermute | solution.py:37
  18.7 3.2 %collective-permute-start.4 = (bf16[2,2,32,896]{3,2,1,0:T(8,128)(2,1)S(1)}, bf16[2,2,32,896]{3,2,1,0:T(8,128)(2,1)S(1)}, u32[]{:S(2)}, u32[]{:S(2)}) collective-permute-start(bf16[2,2,32,896]{3,2,1,0:T(8,128)(2,1)S(1)} %collective-permute-done.2), channel_id=1, source_target_pairs={{0,224},{32,0},{64,32},{96,64},{128,96},{160,128},{192,160},{224,1... | collective-permute-start | bytes 688136 | tf_op jit(solution)/shard_map/ppermute | solution.py:37
  23.3 2.6 %collective-permute-done.3 = bf16[2,2,32,896]{3,2,1,0:T(8,128)(2,1)S(1)} collective-permute-done((bf16[2,2,32,896]{3,2,1,0:T(8,128)(2,1)S(1)}, bf16[2,2,32,896]{3,2,1,0:T(8,128)(2,1)S(1)}, u32[]{:S(2)}, u32[]{:S(2)}) %collective-permute-start.3) | collective-permute-done | bytes 229408 | tf_op jit(solution)/shard_map/ppermute | solution.py:37
  25.9 3.2 %collective-permute-start.6 = (bf16[2,2,32,896]{3,2,1,0:T(8,128)(2,1)S(1)}, bf16[2,2,32,896]{3,2,1,0:T(8,128)(2,1)S(1)}, u32[]{:S(2)}, u32[]{:S(2)}) collective-permute-start(bf16[2,2,32,896]{3,2,1,0:T(8,128)(2,1)S(1)} %collective-permute-done.4), channel_id=1, source_target_pairs={{0,224},{32,0},{64,32},{96,64},{128,96},{160,128},{192,160},{224,1... | collective-permute-start | bytes 688136 | tf_op jit(solution)/shard_map/ppermute | solution.py:37
  30.6 2.6 %collective-permute-done.5 = bf16[2,2,32,896]{3,2,1,0:T(8,128)(2,1)S(1)} collective-permute-done((bf16[2,2,32,896]{3,2,1,0:T(8,128)(2,1)S(1)}, bf16[2,2,32,896]{3,2,1,0:T(8,128)(2,1)S(1)}, u32[]{:S(2)}, u32[]{:S(2)}) %collective-permute-start.5) | collective-permute-done | bytes 229408 | tf_op jit(solution)/shard_map/ppermute | solution.py:37
  33.3 3.4 %collective-permute-start.8 = (bf16[1,2,32,896]{3,2,1,0:T(8,128)(2,1)S(1)}, bf16[1,2,32,896]{3,2,1,0:T(8,128)(2,1)S(1)}, u32[]{:S(2)}, u32[]{:S(2)}) collective-permute-start(bf16[1,2,32,896]{3,2,1,0:T(8,128)(2,1)S(1)} %slice.19), channel_id=1, source_target_pairs={{0,224},{32,0},{64,32},{96,64},{128,96},{160,128},{192,160},{224,1... | collective-permute-start | bytes 344072 | tf_op jit(solution)/shard_map/ppermute | solution.py:37
  46.0 13.8 %forward.1 = (bf16[1024,896]{1,0:T(8,128)(2,1)S(1)}, bf16[1024,896]{1,0:T(8,128)(2,1)S(1)}, bf16[640,896]{1,0:T(8,128)(2,1)S(1)}, bf16[640,896]{1,0:T(8,128)(2,1)S(1)}, s16[8,256,896]{2,1,0:T(8,128)(2,1)}) custom-call(s32[5]{0:T(128)S(1)} %stack.59.place_ref, s32[1,1024]{1,0:T(1,128)S(1)} %reshape_select_fusion.1.pos_ref, ...), custom_call_target="tpu_custom_call" | custom-call | tf_op jit(solution)/shard_map/forward/pallas_call | solution.py:199
  64.4 6.0 %all-to-all-start = ((s16[8,256,896]{2,1,0:T(8,128)(2,1)}), s16[8,256,896]{2,1,0:T(8,128)(2,1)}, u32[]{:S(2)}, u32[]{:S(2)}) async-start(s16[8,256,896]{2,1,0:T(8,128)(2,1)} %get-tuple-element.31), calls=%async_computation | async-start | bytes 7340032 | tf_op jit(solution)/shard_map/all_to_all | solution.py:209
  70.7 51.6 %all-to-all-done.in_ref = s16[8,256,896]{2,1,0:T(8,128)(2,1)} async-done(((s16[8,256,896]{2,1,0:T(8,128)(2,1)}), s16[8,256,896]{2,1,0:T(8,128)(2,1)}, u32[]{:S(2)}, u32[]{:S(2)}) %all-to-all-start) | async-done | bytes 3670048 | tf_op jit(solution)/shard_map/all_to_all | solution.py:209
  122.4 3.1 %terms.1 = (bf16[80,896]{1,0:T(8,128)(2,1)S(1)}, bf16[80,896]{1,0:T(8,128)(2,1)S(1)}, bf16[80,896]{1,0:T(8,128)(2,1)S(1)}) custom-call(s16[8,256,896]{2,1,0:T(8,128)(2,1)} %all-to-all-done.in_ref, f32[1,896]{1,0:T(1,128)S(1)} %broadcast_in_dim.53.weight_ref), custom_call_target="tpu_custom_call" | custom-call | tf_op jit(solution)/shard_map/terms/pallas_call | solution.py:210
  125.5 1.6 collective-permute-start.17
  127.1 2.0 collective-permute-start.11
  129.1 4.0 %collective-permute-start.12 = (bf16[80,896]{1,0:T(8,128)(2,1)S(1)}, bf16[80,896]{1,0:T(8,128)(2,1)S(1)}, u32[]{:S(2)}, u32[]{:S(2)}) collective-permute-start(bf16[80,896]{1,0:T(8,128)(2,1)S(1)} %get-tuple-element.32), channel_id=1, source_target_pairs={{0,2},{1,3},{2,0},{3,1},{4,6},{5,7},{6,4},{7,5},{8,10},{9,11},{10,... | collective-permute-start | bytes 430088 | tf_op jit(solution)/shard_map/ppermute | solution.py:37
  133.7 1.8 collective-permute-start.14
  137.5 2.5 %collective-permute-done.12 = bf16[80,896]{1,0:T(8,128)(2,1)S(1)} collective-permute-done((bf16[80,896]{1,0:T(8,128)(2,1)S(1)}, bf16[80,896]{1,0:T(8,128)(2,1)S(1)}, u32[]{:S(2)}, u32[]{:S(2)}) %collective-permute-start.12) | collective-permute-done | bytes 143392 | tf_op jit(solution)/shard_map/ppermute | solution.py:37
  143.0 3.1 %collective-permute-done.15 = bf16[80,896]{1,0:T(8,128)(2,1)S(1)} collective-permute-done((bf16[80,896]{1,0:T(8,128)(2,1)S(1)}, bf16[80,896]{1,0:T(8,128)(2,1)S(1)}, u32[]{:S(2)}, u32[]{:S(2)}) %collective-permute-start.15) | collective-permute-done | bytes 143392 | tf_op jit(solution)/shard_map/ppermute | solution.py:37
  146.0 1.5 collective-permute-done.16
  147.6 3.0 %collective-permute-done.20.refs_11_ = bf16[2,80,896]{2,1,0:T(8,128)(2,1)S(1)} collective-permute-done((bf16[2,80,896]{2,1,0:T(8,128)(2,1)S(1)}, bf16[2,80,896]{2,1,0:T(8,128)(2,1)S(1)}, u32[]{:S(2)}, u32[]{:S(2)}) %collective-permute-start.20) | collective-permute-done | bytes 286752 | tf_op jit(solution)/shard_map/ppermute | solution.py:37
  150.5 7.4 %input.1 = (f32[16,32,896]{2,1,0:T(8,128)S(1)}, bf16[16,32,896]{2,1,0:T(8,128)(2,1)S(1)}, bf16[640,896]{1,0:T(8,128)(2,1)S(1)}, bf16[640,896]{1,0:T(8,128)(2,1)S(1)}) custom-call(s32[5]{0:T(128)S(1)} %stack.59.place_ref, s32[1024,1]{1,0:T(8,128)S(1)} %reshape_select_fusion.pos_ref, bf16[1,80,896]{2,1,0:T(8,128)(2,1)S(1)} %bitcast.46, ...), custom_call_target="tpu_custom_call" | custom-call | tf_op jit(solution)/shard_map/input/pallas_call | solution.py:219
  159.9 2.5 %collective-permute-done.21 = bf16[16,32,896]{2,1,0:T(8,128)(2,1)S(1)} collective-permute-done((bf16[16,32,896]{2,1,0:T(8,128)(2,1)S(1)}, bf16[16,32,896]{2,1,0:T(8,128)(2,1)S(1)}, u32[]{:S(2)}, u32[]{:S(2)}) %collective-permute-start.21) | collective-permute-done | bytes 917536 | tf_op jit(solution)/shard_map/ppermute | solution.py:37
  163.6 8.6 %all-to-all-start.1 = ((bf16[16,32,896]{2,1,0:T(8,128)(2,1)}), bf16[16,32,896]{2,1,0:T(8,128)(2,1)}, u32[]{:S(2)}, u32[]{:S(2)}) async-start(bf16[16,32,896]{2,1,0:T(8,128)(2,1)} %add_convert_fusion), calls=%async_computation.1 | async-start | bytes 1835008 | tf_op jit(solution)/shard_map/all_to_all | solution.py:230
  172.2 5.5 %collective-permute-done.22 = bf16[80,896]{1,0:T(8,128)(2,1)S(1)} collective-permute-done((bf16[80,896]{1,0:T(8,128)(2,1)S(1)}, bf16[80,896]{1,0:T(8,128)(2,1)S(1)}, u32[]{:S(2)}, u32[]{:S(2)}) %collective-permute-start.22) | collective-permute-done | bytes 143392 | tf_op jit(solution)/shard_map/ppermute | solution.py:37
  177.9 2.0 collective-permute-start.24
  179.9 2.3 %collective-permute-start.25 = (bf16[2,80,896]{2,1,0:T(8,128)(2,1)S(1)}, bf16[2,80,896]{2,1,0:T(8,128)(2,1)S(1)}, u32[]{:S(2)}, u32[]{:S(2)}) collective-permute-start(bf16[2,80,896]{2,1,0:T(8,128)(2,1)S(1)} %pad_maximum_fusion.1.refs_0_), channel_id=1, source_target_pairs={{0,2},{1,3},{2,0},{3,1},{4,6},{5,7},{6,4},{7,5},{8,10},{9,11},{10,... | collective-permute-start | bytes 860168 | tf_op jit(solution)/shard_map/ppermute | solution.py:37
  182.2 5.4 %collective-permute-done.23.refs_1_ = bf16[2,80,896]{2,1,0:T(8,128)(2,1)S(1)} collective-permute-done((bf16[2,80,896]{2,1,0:T(8,128)(2,1)S(1)}, bf16[2,80,896]{2,1,0:T(8,128)(2,1)S(1)}, u32[]{:S(2)}, u32[]{:S(2)}) %collective-permute-start.23) | collective-permute-done | bytes 286752 | tf_op jit(solution)/shard_map/ppermute | solution.py:37
  187.6 6.1 %collective-permute-done.25.refs_3_ = bf16[2,80,896]{2,1,0:T(8,128)(2,1)S(1)} collective-permute-done((bf16[2,80,896]{2,1,0:T(8,128)(2,1)S(1)}, bf16[2,80,896]{2,1,0:T(8,128)(2,1)S(1)}, u32[]{:S(2)}, u32[]{:S(2)}) %collective-permute-start.25) | collective-permute-done | bytes 286752 | tf_op jit(solution)/shard_map/ppermute | solution.py:37
  199.0 6.5 %weights.1 = (f32[152,896]{1,0:T(8,128)}, f32[152,896]{1,0:T(8,128)}, f32[152,896]{1,0:T(8,128)}, f32[608,896]{1,0:T(8,128)}, f32[608,896]{1,0:T(8,128)}, /*index=5*/f32[608,896]{1,0:T(8,128)}) custom-call(s32[5]{0:T(128)S(1)} %stack.59.place_ref, bf16[640,896]{1,0:T(8,128)(2,1)S(1)} %copy-done.11, bf16[640,896]{1,0:T(8,128)(2,1)S(1)} %copy-done.13, ...), custom_call_target="tpu_custom_call" | custom-call | tf_op jit(solution)/shard_map/weights/pallas_call | solution.py:232
  205.5 2.0 convert_reduce_fusion
  (101 shorter events, 34.5 us)
Async XLA Ops:
  1.5 6.5 %collective-permute-start = (bf16[2,32,896]{2,1,0:T(8,128)(2,1)S(1)}, bf16[2,32,896]{2,1,0:T(8,128)(2,1)S(1)}, u32[]{:S(2)}, u32[]{:S(2)}) collective-permute-start(bf16[2,32,896]{2,1,0:T(8,128)(2,1)S(1)} %get-tuple-element.54), channel_id=1, source_target_pairs={{0,16},{16,0},{1,17},{17,1},{2,18},{18,2},{3,19},{19,3},{4,20},{20... | collective-permute-start | bytes 344072 | tf_op jit(solution)/shard_map/ppermute | solution.py:37
  8.0 10.7 %collective-permute-start.1 = (bf16[2,2,32,896]{3,2,1,0:T(8,128)(2,1)S(1)}, bf16[2,2,32,896]{3,2,1,0:T(8,128)(2,1)S(1)}, u32[]{:S(2)}, u32[]{:S(2)}) collective-permute-start(bf16[2,2,32,896]{3,2,1,0:T(8,128)(2,1)S(1)} %pad_maximum_fusion.2), channel_id=1, source_target_pairs={{0,32},{32,64},{64,96},{96,128},{128,160},{160,192},{192,224},{224... | collective-permute-start | bytes 688136 | tf_op jit(solution)/shard_map/ppermute | solution.py:37
  10.0 8.7 %collective-permute-start.2 = (bf16[2,2,32,896]{3,2,1,0:T(8,128)(2,1)S(1)}, bf16[2,2,32,896]{3,2,1,0:T(8,128)(2,1)S(1)}, u32[]{:S(2)}, u32[]{:S(2)}) collective-permute-start(bf16[2,2,32,896]{3,2,1,0:T(8,128)(2,1)S(1)} %pad_maximum_fusion.2), channel_id=1, source_target_pairs={{0,224},{32,0},{64,32},{96,64},{128,96},{160,128},{192,160},{224,1... | collective-permute-start | bytes 688136 | tf_op jit(solution)/shard_map/ppermute | solution.py:37
  14.7 25.9 %copy-start.18 = (s32[1024,2]{0,1:T(2,128)S(1)}, s32[1024,2]{0,1:T(2,128)}, u32[]{:S(2)}) copy-start(s32[1024,2]{0,1:T(2,128)} %param.12) | copy-start | bytes 24580
  18.7 7.2 %collective-permute-start.3 = (bf16[2,2,32,896]{3,2,1,0:T(8,128)(2,1)S(1)}, bf16[2,2,32,896]{3,2,1,0:T(8,128)(2,1)S(1)}, u32[]{:S(2)}, u32[]{:S(2)}) collective-permute-start(bf16[2,2,32,896]{3,2,1,0:T(8,128)(2,1)S(1)} %collective-permute-done.1), channel_id=1, source_target_pairs={{0,32},{32,64},{64,96},{96,128},{128,160},{160,192},{192,224},{224... | collective-permute-start | bytes 688136 | tf_op jit(solution)/shard_map/ppermute | solution.py:37
  18.7 7.2 %collective-permute-start.4 = (bf16[2,2,32,896]{3,2,1,0:T(8,128)(2,1)S(1)}, bf16[2,2,32,896]{3,2,1,0:T(8,128)(2,1)S(1)}, u32[]{:S(2)}, u32[]{:S(2)}) collective-permute-start(bf16[2,2,32,896]{3,2,1,0:T(8,128)(2,1)S(1)} %collective-permute-done.2), channel_id=1, source_target_pairs={{0,224},{32,0},{64,32},{96,64},{128,96},{160,128},{192,160},{224,1... | collective-permute-start | bytes 688136 | tf_op jit(solution)/shard_map/ppermute | solution.py:37
  25.9 7.2 %collective-permute-start.5 = (bf16[2,2,32,896]{3,2,1,0:T(8,128)(2,1)S(1)}, bf16[2,2,32,896]{3,2,1,0:T(8,128)(2,1)S(1)}, u32[]{:S(2)}, u32[]{:S(2)}) collective-permute-start(bf16[2,2,32,896]{3,2,1,0:T(8,128)(2,1)S(1)} %collective-permute-done.3), channel_id=1, source_target_pairs={{0,32},{32,64},{64,96},{96,128},{128,160},{160,192},{192,224},{224... | collective-permute-start | bytes 688136 | tf_op jit(solution)/shard_map/ppermute | solution.py:37
  25.9 7.3 %collective-permute-start.6 = (bf16[2,2,32,896]{3,2,1,0:T(8,128)(2,1)S(1)}, bf16[2,2,32,896]{3,2,1,0:T(8,128)(2,1)S(1)}, u32[]{:S(2)}, u32[]{:S(2)}) collective-permute-start(bf16[2,2,32,896]{3,2,1,0:T(8,128)(2,1)S(1)} %collective-permute-done.4), channel_id=1, source_target_pairs={{0,224},{32,0},{64,32},{96,64},{128,96},{160,128},{192,160},{224,1... | collective-permute-start | bytes 688136 | tf_op jit(solution)/shard_map/ppermute | solution.py:37
  30.6 14.1 %copy-start.17 = (bf16[152,896]{1,0:T(8,128)(2,1)S(1)}, bf16[152,896]{1,0:T(8,128)(2,1)}, u32[]{:S(2)}) copy-start(bf16[152,896]{1,0:T(8,128)(2,1)} %refs_5_.1) | copy-start | bytes 817156
  33.2 6.1 %collective-permute-start.7 = (bf16[1,2,32,896]{3,2,1,0:T(8,128)(2,1)S(1)}, bf16[1,2,32,896]{3,2,1,0:T(8,128)(2,1)S(1)}, u32[]{:S(2)}, u32[]{:S(2)}) collective-permute-start(bf16[1,2,32,896]{3,2,1,0:T(8,128)(2,1)S(1)} %slice.18), channel_id=1, source_target_pairs={{0,32},{32,64},{64,96},{96,128},{128,160},{160,192},{192,224},{224... | collective-permute-start | bytes 344072 | tf_op jit(solution)/shard_map/ppermute | solution.py:37
  33.3 6.6 %collective-permute-start.8 = (bf16[1,2,32,896]{3,2,1,0:T(8,128)(2,1)S(1)}, bf16[1,2,32,896]{3,2,1,0:T(8,128)(2,1)S(1)}, u32[]{:S(2)}, u32[]{:S(2)}) collective-permute-start(bf16[1,2,32,896]{3,2,1,0:T(8,128)(2,1)S(1)} %slice.19), channel_id=1, source_target_pairs={{0,224},{32,0},{64,32},{96,64},{128,96},{160,128},{192,160},{224,1... | collective-permute-start | bytes 344072 | tf_op jit(solution)/shard_map/ppermute | solution.py:37
  40.6 4.1 %collective-permute-start.9 = (bf16[16,2,32,896]{3,2,1,0:T(8,128)(2,1)}, bf16[16,2,32,896]{3,2,1,0:T(8,128)(2,1)}, u32[]{:S(2)}, u32[]{:S(2)}) collective-permute-start(bf16[16,2,32,896]{3,2,1,0:T(8,128)(2,1)} %constant_dynamic-update-slice_fusion.mine_ref), channel_id=1, source_target_pairs={{0,8},{8,0},{1,9},{9,1},{2,10},{10,2},{3,11},{11,3},{4,12},{12,4},... | collective-permute-start | bytes 5505032 | tf_op jit(solution)/shard_map/ppermute | solution.py:37
  64.4 58.0 %all-to-all-start = ((s16[8,256,896]{2,1,0:T(8,128)(2,1)}), s16[8,256,896]{2,1,0:T(8,128)(2,1)}, u32[]{:S(2)}, u32[]{:S(2)}) async-start(s16[8,256,896]{2,1,0:T(8,128)(2,1)} %get-tuple-element.31), calls=%async_computation | async-start | bytes 7340032 | tf_op jit(solution)/shard_map/all_to_all | solution.py:209
  125.5 8.2 %collective-permute-start.17 = (bf16[80,896]{1,0:T(8,128)(2,1)S(1)}, bf16[80,896]{1,0:T(8,128)(2,1)S(1)}, u32[]{:S(2)}, u32[]{:S(2)}) collective-permute-start(bf16[80,896]{1,0:T(8,128)(2,1)S(1)} %get-tuple-element.33), channel_id=1, source_target_pairs={{0,4},{4,0},{1,5},{5,1},{2,6},{6,2},{3,7},{7,3},{8,12},{12,8},{9,1... | collective-permute-start | bytes 430088 | tf_op jit(solution)/shard_map/ppermute | solution.py:37
  127.1 6.7 %collective-permute-start.10 = (bf16[80,896]{1,0:T(8,128)(2,1)S(1)}, bf16[80,896]{1,0:T(8,128)(2,1)S(1)}, u32[]{:S(2)}, u32[]{:S(2)}) collective-permute-start(bf16[80,896]{1,0:T(8,128)(2,1)S(1)} %get-tuple-element.32), channel_id=1, source_target_pairs={{0,1},{1,2},{2,3},{3,0},{4,5},{5,6},{6,7},{7,4},{8,9},{9,10},{10,1... | collective-permute-start | bytes 430088 | tf_op jit(solution)/shard_map/ppermute | solution.py:37
  127.1 9.5 %collective-permute-start.11 = (bf16[80,896]{1,0:T(8,128)(2,1)S(1)}, bf16[80,896]{1,0:T(8,128)(2,1)S(1)}, u32[]{:S(2)}, u32[]{:S(2)}) collective-permute-start(bf16[80,896]{1,0:T(8,128)(2,1)S(1)} %get-tuple-element.32), channel_id=1, source_target_pairs={{0,3},{1,0},{2,1},{3,2},{4,7},{5,4},{6,5},{7,6},{8,11},{9,8},{10,9... | collective-permute-start | bytes 430088 | tf_op jit(solution)/shard_map/ppermute | solution.py:37
  129.1 11.0 %collective-permute-start.12 = (bf16[80,896]{1,0:T(8,128)(2,1)S(1)}, bf16[80,896]{1,0:T(8,128)(2,1)S(1)}, u32[]{:S(2)}, u32[]{:S(2)}) collective-permute-start(bf16[80,896]{1,0:T(8,128)(2,1)S(1)} %get-tuple-element.32), channel_id=1, source_target_pairs={{0,2},{1,3},{2,0},{3,1},{4,6},{5,7},{6,4},{7,5},{8,10},{9,11},{10,... | collective-permute-start | bytes 430088 | tf_op jit(solution)/shard_map/ppermute | solution.py:37
  133.1 7.8 %collective-permute-start.13 = (bf16[80,896]{1,0:T(8,128)(2,1)S(1)}, bf16[80,896]{1,0:T(8,128)(2,1)S(1)}, u32[]{:S(2)}, u32[]{:S(2)}) collective-permute-start(bf16[80,896]{1,0:T(8,128)(2,1)S(1)} %get-tuple-element.32), channel_id=1, source_target_pairs={{0,4},{4,0},{1,5},{5,1},{2,6},{6,2},{3,7},{7,3},{8,12},{12,8},{9,1... | collective-permute-start | bytes 430088 | tf_op jit(solution)/shard_map/ppermute | solution.py:37
  133.7 8.0 %collective-permute-start.14 = (bf16[80,896]{1,0:T(8,128)(2,1)S(1)}, bf16[80,896]{1,0:T(8,128)(2,1)S(1)}, u32[]{:S(2)}, u32[]{:S(2)}) collective-permute-start(bf16[80,896]{1,0:T(8,128)(2,1)S(1)} %collective-permute-done.10), channel_id=1, source_target_pairs={{0,4},{4,0},{1,5},{5,1},{2,6},{6,2},{3,7},{7,3},{8,12},{12,8},{9,1... | collective-permute-start | bytes 430088 | tf_op jit(solution)/shard_map/ppermute | solution.py:37
  135.5 12.1 %collective-permute-start.18 = (bf16[2,80,896]{2,1,0:T(8,128)(2,1)S(1)}, bf16[2,80,896]{2,1,0:T(8,128)(2,1)S(1)}, u32[]{:S(2)}, u32[]{:S(2)}) collective-permute-start(bf16[2,80,896]{2,1,0:T(8,128)(2,1)S(1)} %pad_maximum_fusion.refs_8_), channel_id=1, source_target_pairs={{0,1},{1,2},{2,3},{3,0},{4,5},{5,6},{6,7},{7,4},{8,9},{9,10},{10,1... | collective-permute-start | bytes 860168 | tf_op jit(solution)/shard_map/ppermute | solution.py:37
  136.5 11.1 %collective-permute-start.19 = (bf16[2,80,896]{2,1,0:T(8,128)(2,1)S(1)}, bf16[2,80,896]{2,1,0:T(8,128)(2,1)S(1)}, u32[]{:S(2)}, u32[]{:S(2)}) collective-permute-start(bf16[2,80,896]{2,1,0:T(8,128)(2,1)S(1)} %pad_maximum_fusion.refs_8_), channel_id=1, source_target_pairs={{0,3},{1,0},{2,1},{3,2},{4,7},{5,4},{6,5},{7,6},{8,11},{9,8},{10,9... | collective-permute-start | bytes 860168 | tf_op jit(solution)/shard_map/ppermute | solution.py:37
  140.1 10.5 %collective-permute-start.20 = (bf16[2,80,896]{2,1,0:T(8,128)(2,1)S(1)}, bf16[2,80,896]{2,1,0:T(8,128)(2,1)S(1)}, u32[]{:S(2)}, u32[]{:S(2)}) collective-permute-start(bf16[2,80,896]{2,1,0:T(8,128)(2,1)S(1)} %pad_maximum_fusion.refs_8_), channel_id=1, source_target_pairs={{0,2},{1,3},{2,0},{3,1},{4,6},{5,7},{6,4},{7,5},{8,10},{9,11},{10,... | collective-permute-start | bytes 860168 | tf_op jit(solution)/shard_map/ppermute | solution.py:37
  140.9 5.1 %collective-permute-start.15 = (bf16[80,896]{1,0:T(8,128)(2,1)S(1)}, bf16[80,896]{1,0:T(8,128)(2,1)S(1)}, u32[]{:S(2)}, u32[]{:S(2)}) collective-permute-start(bf16[80,896]{1,0:T(8,128)(2,1)S(1)} %collective-permute-done.11), channel_id=1, source_target_pairs={{0,4},{4,0},{1,5},{5,1},{2,6},{6,2},{3,7},{7,3},{8,12},{12,8},{9,1... | collective-permute-start | bytes 430088 | tf_op jit(solution)/shard_map/ppermute | solution.py:37
  141.7 5.8 %collective-permute-start.16 = (bf16[80,896]{1,0:T(8,128)(2,1)S(1)}, bf16[80,896]{1,0:T(8,128)(2,1)S(1)}, u32[]{:S(2)}, u32[]{:S(2)}) collective-permute-start(bf16[80,896]{1,0:T(8,128)(2,1)S(1)} %collective-permute-done.12), channel_id=1, source_target_pairs={{0,4},{4,0},{1,5},{5,1},{2,6},{6,2},{3,7},{7,3},{8,12},{12,8},{9,1... | collective-permute-start | bytes 430088 | tf_op jit(solution)/shard_map/ppermute | solution.py:37
  159.9 2.5 %collective-permute-start.21 = (bf16[16,32,896]{2,1,0:T(8,128)(2,1)S(1)}, bf16[16,32,896]{2,1,0:T(8,128)(2,1)S(1)}, u32[]{:S(2)}, u32[]{:S(2)}) collective-permute-start(bf16[16,32,896]{2,1,0:T(8,128)(2,1)S(1)} %get-tuple-element.37), channel_id=1, source_target_pairs={{0,8},{8,0},{1,9},{9,1},{2,10},{10,2},{3,11},{11,3},{4,12},{12,4},... | collective-permute-start | bytes 2752520 | tf_op jit(solution)/shard_map/ppermute | solution.py:37
  162.4 31.4 %copy-start.7 = (bf16[640,896]{1,0:T(8,128)(2,1)S(1)}, bf16[640,896]{1,0:T(8,128)(2,1)}, u32[]{:S(2)}) copy-start(bf16[640,896]{1,0:T(8,128)(2,1)} %copy-done.6) | copy-start | bytes 3440644
  163.6 30.2 %copy-start.3 = (bf16[1024,896]{1,0:T(8,128)(2,1)S(1)}, bf16[1024,896]{1,0:T(8,128)(2,1)}, u32[]{:S(2)}) copy-start(bf16[1024,896]{1,0:T(8,128)(2,1)} %copy-done.2) | copy-start | bytes 5505028
  163.6 41.9 %all-to-all-start.1 = ((bf16[16,32,896]{2,1,0:T(8,128)(2,1)}), bf16[16,32,896]{2,1,0:T(8,128)(2,1)}, u32[]{:S(2)}, u32[]{:S(2)}) async-start(bf16[16,32,896]{2,1,0:T(8,128)(2,1)} %add_convert_fusion), calls=%async_computation.1 | async-start | bytes 1835008 | tf_op jit(solution)/shard_map/all_to_all | solution.py:230
  172.1 5.6 %collective-permute-start.22 = (bf16[80,896]{1,0:T(8,128)(2,1)S(1)}, bf16[80,896]{1,0:T(8,128)(2,1)S(1)}, u32[]{:S(2)}, u32[]{:S(2)}) collective-permute-start(bf16[80,896]{1,0:T(8,128)(2,1)S(1)} %get-tuple-element.40), channel_id=1, source_target_pairs={{0,4},{4,0},{1,5},{5,1},{2,6},{6,2},{3,7},{7,3},{8,12},{12,8},{9,1... | collective-permute-start | bytes 430088 | tf_op jit(solution)/shard_map/ppermute | solution.py:37
  177.8 9.8 %collective-permute-start.23 = (bf16[2,80,896]{2,1,0:T(8,128)(2,1)S(1)}, bf16[2,80,896]{2,1,0:T(8,128)(2,1)S(1)}, u32[]{:S(2)}, u32[]{:S(2)}) collective-permute-start(bf16[2,80,896]{2,1,0:T(8,128)(2,1)S(1)} %pad_maximum_fusion.1.refs_0_), channel_id=1, source_target_pairs={{0,1},{1,2},{2,3},{3,0},{4,5},{5,6},{6,7},{7,4},{8,9},{9,10},{10,1... | collective-permute-start | bytes 860168 | tf_op jit(solution)/shard_map/ppermute | solution.py:37
  177.9 9.7 %collective-permute-start.24 = (bf16[2,80,896]{2,1,0:T(8,128)(2,1)S(1)}, bf16[2,80,896]{2,1,0:T(8,128)(2,1)S(1)}, u32[]{:S(2)}, u32[]{:S(2)}) collective-permute-start(bf16[2,80,896]{2,1,0:T(8,128)(2,1)S(1)} %pad_maximum_fusion.1.refs_0_), channel_id=1, source_target_pairs={{0,3},{1,0},{2,1},{3,2},{4,7},{5,4},{6,5},{7,6},{8,11},{9,8},{10,9... | collective-permute-start | bytes 860168 | tf_op jit(solution)/shard_map/ppermute | solution.py:37
  179.9 13.9 %collective-permute-start.25 = (bf16[2,80,896]{2,1,0:T(8,128)(2,1)S(1)}, bf16[2,80,896]{2,1,0:T(8,128)(2,1)S(1)}, u32[]{:S(2)}, u32[]{:S(2)}) collective-permute-start(bf16[2,80,896]{2,1,0:T(8,128)(2,1)S(1)} %pad_maximum_fusion.1.refs_0_), channel_id=1, source_target_pairs={{0,2},{1,3},{2,0},{3,1},{4,6},{5,7},{6,4},{7,5},{8,10},{9,11},{10,... | collective-permute-start | bytes 860168 | tf_op jit(solution)/shard_map/ppermute | solution.py:37
  (16 other events, 75.6 us)
